TPU v7x, 32 devices: a whole 2x2x4 slice. The times are simulated.
32 devices in a mesh: dom: 8 (over z, y), rep: 4 (over x, core).
Axes of the slice: x: 2, y: 2, z: 4, core: 2. Of those that a mesh axis runs over, the one named last changes fastest.
Arguments:
- coords: float32 [8, 3, 8192], P('dom'), may hold values from -6 to 6
- disp: float32 [8, 3, 8192], P('dom'), may hold values from -4 to 4
- mass: float32 [8, 8192], P('dom'), may hold values from 0.5 to 4
- stiffness: float32 [24, 24], replicated, may hold values from -1.25 to 1.25
- elem_nodes: int32 [8, 8, 4096], P('dom', None, 'rep'), may hold values from 0 to 8191
- modulus: float32 [8, 4096], P('dom', 'rep'), may hold values from 0.3 to 3
- surf_nodes: int32 [8, 128, 128], P('dom'), may hold values from 0 to 8191
- block_region: int32 [8, 128], P('dom'), may hold values from 0 to 7, as said below
- face_pos: float32 [8, 64, 3, 128], P('dom'), may hold values from -6 to 6
- face_normal: float32 [8, 64, 3, 128], P('dom'), may hold values from -6 to 6
- tile_slot: int32 [8, 32], P('dom', 'rep'), may hold values from 0 to 255, as said below
- tile_face: int32 [8, 32], P('dom', 'rep'), may hold values from 0 to 63
- tile_weight: bfloat16 [8, 32, 128, 128], P('dom', 'rep'), may hold values from -0.5 to 0.5
- shared_lo: int32 [8, 512], P('dom'), may hold values from 0 to 8191
- shared_hi: int32 [8, 512], P('dom'), may hold values from 0 to 8191
Outputs:
- accel: float32 [8, 3, 8192], P('dom')
Inputs may be any that keep to these rules, and one draw needn't show every extreme that they name: `block_region`: each partition's blocks come in runs of 32: blocks b with equal b // 32 share a box, and the 4 runs go to distinct boxes, so a partition sends at most 32 blocks to one box. Partition s always sends a run to each of the boxes s + 1, s - 1 and s + 8 // 2 (counted round). `tile_slot`: slot source * 32 + c with c < 32, where the source partition sends blocks to this box.
All inputs are finite; a program needn't handle non-finite values.
Results may differ from a plain program's by a relative error of at most 0.0065.
Values may be sent and summed in bfloat16 or wider, within the bound.
No kernel may reach another device: no remote copies, remote signals or barrier semaphores. Data moves between devices by JAX's collectives and lax.ppermute only.
A program may use at most 64 MiB of HBM per device.

v0:
```python
import jax
import jax.numpy as jnp
from jax import lax
from jax.sharding import PartitionSpec as P

penalty = 4.0


def shifted(block, axis, distance):
    devices = range(lax.axis_size(axis))
    route = [(i - distance, i) for i in devices if i - distance in devices]
    return lax.ppermute(block, axis, route)


def on_device(
    coords,
    disp,
    mass,
    stiffness,
    elem_nodes,
    modulus,
    surf_nodes,
    block_region,
    face_pos,
    face_normal,
    tile_slot,
    tile_face,
    tile_weight,
    shared_lo,
    shared_hi,
):
    parts = lax.axis_size("dom")
    moved = disp[0]
    positions = coords[0] + moved
    surf = surf_nodes[0]
    nblk = surf.shape[0]
    width = surf.shape[1]
    nodes_all = moved.shape[1]
    cap = max(2, 2 * nblk // parts)
    boxes = block_region[0]
    order = jnp.arange(nblk, dtype=jnp.int32)
    same = boxes[None, :] == boxes[:, None]
    rank = jnp.sum(same & (order[None, :] < order[:, None]), axis=1)
    target = boxes * cap + rank
    blocks = jnp.moveaxis(jnp.take(positions, surf, axis=1), 1, 0).astype(jnp.bfloat16)
    outgoing = jnp.zeros((parts * cap, 3, width), jnp.bfloat16).at[target].set(blocks)
    arrived = lax.all_to_all(
        outgoing.reshape(parts, cap, 3, width), "dom", split_axis=0, concat_axis=0, tiled=True
    )
    received = arrived.reshape(parts * cap, 3, width)
    slot = tile_slot[0]
    face = tile_face[0]
    weights = tile_weight[0]
    xs = received[slot]
    pf = face_pos[0][face]
    nf = face_normal[0][face]
    interp = jnp.einsum("tck,tik->tci", xs, weights, preferred_element_type=jnp.float32)
    gap = jnp.sum(nf * (interp - pf), axis=1)
    pressure = penalty * jnp.maximum(-gap, 0.0)
    push = (pressure[:, None, :] * nf).astype(jnp.bfloat16)
    tile_force = jnp.einsum("tci,tik->tck", push, weights, preferred_element_type=jnp.float32)
    partial_force = jnp.zeros((parts * cap, 3, width), jnp.float32).at[slot].add(tile_force)
    partial_force = partial_force.reshape(parts, cap, 3, width)
    corner_points = elem_nodes[0]
    local = moved[:, corner_points].reshape(24, -1)
    elem_force = jnp.dot(stiffness, local, precision=lax.Precision.HIGHEST) * modulus[0][None, :]
    returned = lax.all_to_all(partial_force, "dom", split_axis=0, concat_axis=0, tiled=True)
    block_force = returned.reshape(parts * cap, 3, width)[target]
    node_index = jnp.concatenate([surf.reshape(-1), corner_points.reshape(-1)])
    node_terms = jnp.concatenate(
        [jnp.moveaxis(block_force, 0, 1).reshape(3, -1), -elem_force.reshape(3, -1)], axis=1
    )
    local_sum = jnp.zeros((3, nodes_all), jnp.float32).at[:, node_index].add(node_terms)
    own = lax.psum(local_sum, "rep")
    full = jnp.concatenate([own, mass[0][None, :]], axis=0)
    lower_nodes = shared_lo[0]
    upper_nodes = shared_hi[0]
    from_upper = shifted(full[:, lower_nodes], "dom", -1)
    from_lower = shifted(full[:, upper_nodes], "dom", 1)
    total = full.at[:, upper_nodes].add(from_upper).at[:, lower_nodes].add(from_lower)
    return (total[:3] / total[3:])[None]


def solution(mesh):
    in_specs = (
        P("dom", None, None),
        P("dom", None, None),
        P("dom", None),
        P(),
        P("dom", None, "rep"),
        P("dom", "rep"),
        P("dom", None, None),
        P("dom", None),
        P("dom", None, None, None),
        P("dom", None, None, None),
        P("dom", "rep"),
        P("dom", "rep"),
        P("dom", "rep", None, None),
        P("dom", None),
        P("dom", None),
    )
    out_specs = P("dom", None, None)
    return jax.shard_map(
        on_device, mesh=mesh, in_specs=in_specs, out_specs=out_specs, check_vma=False
    )
```

profile of v0, /device:TPU:0, one launch (start us, length us, event | category | flops | bytes accessed | tf_op | source)
XLA Modules:
  0.0 426.3 jit_solution(15262982919361170333)
XLA Ops:
  6.5 0.9 fusion.17
  7.4 0.9 compare_and_fusion
  8.3 3.4 copy.92
  11.7 2.6 copy.91
  14.3 3.9 bitcast_add_fusion
  18.3 57.4 %gather_fusion.1 = bf16[16384,3]{1,0:T(8,128)(2,1)} fusion(bf16[3,8192]{0,1:T(8,128)(2,1)S(1)} %bitcast_add_fusion, s32[16384]{0:T(1024)S(1)} %fusion.17), kind=kCustom, calls=%fused_computation.1 | custom fusion | bytes 262144 | tf_op jit(solution)/shard_map/jit(_take)/gather | solution.py:45
  75.7 3.9 copy.93
  80.0 4.3 %scatter_fusion = bf16[256,3,128]{2,1,0:T(4,128)(2,1)S(1)} fusion(bf16[256,3,128]{2,1,0:T(4,128)(2,1)S(1)} %broadcast_in_dim.20, s32[128]{0:T(128)S(1)} %fusion.23, bf16[128,3,128]{2,1,0:T(4,128)(2,1)S(1)} %fusion.14), kind=kCustom, calls=%fused_computation.8 | custom fusion | bytes 295424 | tf_op jit(solution)/shard_map/scatter | solution.py:46
  84.4 0.7 copy.94
  85.1 7.3 %all-to-all-start = ((bf16[8,32,3,128]{3,1,2,0:T(8,128)(2,1)}), bf16[8,32,3,128]{3,1,2,0:T(8,128)(2,1)S(1)}, u32[]{:S(2)}, u32[]{:S(2)}) async-start(bf16[8,32,3,128]{3,1,2,0:T(8,128)(2,1)} %copy.94), calls=%async_computation | async-start | bytes 393216 | tf_op jit(solution)/shard_map/all_to_all | solution.py:47
  93.9 29.9 %gather_fusion.5 = f32[8192,3]{1,0:T(8,128)} fusion(f32[3,8192]{0,1:T(8,128)} %bitcast.93, s32[8192]{0:T(1024)S(1)} %bitcast_clamp_fusion), kind=kCustom, calls=%fused_computation.5 | custom fusion | bytes 229376 | tf_op jit(solution)/shard_map/gather | solution.py:65
  123.9 2.9 copy.101
  127.0 0.6 gather_fusion.2
  128.1 0.8 scatter_fusion.1
  128.9 0.8 copy.99
  129.7 6.0 %all-to-all-start.1 = ((f32[8,32,3,128]{3,1,2,0:T(8,128)}), f32[8,32,3,128]{3,1,2,0:T(8,128)S(1)}, u32[]{:S(2)}, u32[]{:S(2)}) async-start(f32[8,32,3,128]{3,1,2,0:T(8,128)} %copy.99), calls=%async_computation.1 | async-start | bytes 786432 | tf_op jit(solution)/shard_map/all_to_all | solution.py:67
  136.1 10.7 %all-to-all-done.1 = f32[8,32,3,128]{3,1,2,0:T(8,128)S(1)} async-done(((f32[8,32,3,128]{3,1,2,0:T(8,128)}), f32[8,32,3,128]{3,1,2,0:T(8,128)S(1)}, u32[]{:S(2)}, u32[]{:S(2)}) %all-to-all-start.1) | async-done | bytes 393248 | tf_op jit(solution)/shard_map/all_to_all | solution.py:67
  147.1 0.8 gather_fusion.4
  147.9 7.0 %copy.102 = f32[24576,3]{1,0:T(8,128)} copy(f32[24576,3]{0,1:T(4,128)S(1)} %maximum_bitcast_fusion) | data formatting | bytes 589824 | tf_op jit(solution)/shard_map/concatenate | solution.py:70
  154.9 133.1 %scatter_custom_fusion.2 = f32[3,8192]{0,1:T(8,128)} fusion(s32[24576]{0:T(1024)S(1)} %bitcast.106, f32[24576,3]{1,0:T(8,128)} %copy.102, f32[]{:T(128)} %constant.10.clone.1), kind=kCustom, calls=%fused_computation.18 | custom fusion | flops 73728 | bytes 98816 | tf_op jit(solution)/shard_map/scatter-add | solution.py:73
  288.1 2.7 copy.103
  290.8 82.1 %all-reduce.2.cloned.1.call-done = f32[3,8192]{0,1:T(8,128)} async-done(((f32[3,8192]{0,1:T(8,128)}), f32[3,8192]{0,1:T(8,128)}) %all-reduce.2.cloned.1.call-update) | async-done | bytes 98320 | tf_op jit(solution)/shard_map/psum | solution.py:74
  372.8 6.6 %pad_maximum_fusion = f32[4,8192]{0,1:T(8,128)} fusion(f32[1,8192]{0,1:T(8,128)} %copy.103, f32[3,8192]{0,1:T(8,128)} %all-reduce.2.cloned.1.call-done), kind=kLoop, calls=%fused_computation.16 | loop fusion | flops 32768 | bytes 262144 | tf_op jit(solution)/shard_map/concatenate | solution.py:75
  379.4 3.2 gather_fusion.6
  382.6 1.3 collective-permute-start
  383.9 3.2 gather_fusion.7
  387.1 4.7 %collective-permute-start.1 = (f32[4,512]{0,1:T(8,128)S(1)}, f32[4,512]{0,1:T(8,128)S(1)}, u32[]{:S(2)}, u32[]{:S(2)}) collective-permute-start(f32[4,512]{0,1:T(8,128)S(1)} %bitcast.112), channel_id=1, source_target_pairs={{0,4},{4,8},{8,12},{12,16},{16,20},{20,24},{24,28},{1,5},{5,9},{9,... | collective-permute-start | bytes 24584 | tf_op jit(solution)/shard_map/ppermute | solution.py:12
  392.4 7.2 %scatter_custom_fusion.3 = f32[4,8192]{0,1:T(8,128)} fusion(f32[4,8192]{0,1:T(8,128)} %pad_maximum_fusion, s32[512]{0:T(512)S(1)} %bitcast.110, f32[4,512]{0,1:T(8,128)S(1)} %collective-permute-done), kind=kCustom, calls=%fused_computation.30 | custom fusion | flops 2048 | bytes 393216 | tf_op jit(solution)/shard_map/scatter-add | solution.py:80
  399.6 7.2 %scatter_custom_fusion.4 = f32[4,8192]{0,1:T(8,128)} fusion(f32[4,8192]{0,1:T(8,128)} %scatter_custom_fusion.3, s32[512]{0:T(512)S(1)} %bitcast.108, f32[4,512]{0,1:T(8,128)S(1)} %collective-permute-done.1), kind=kCustom, calls=%fused_computation.28 | custom fusion | flops 2048 | bytes 393216 | tf_op jit(solution)/shard_map/scatter-add | solution.py:80
  406.8 4.6 %slice_reduce_fusion = f32[8192]{0:T(1024)S(1)} fusion(f32[4,8192]{0,1:T(8,128)} %scatter_custom_fusion.4), kind=kLoop, calls=%fused_computation.13 | loop fusion | bytes 65536 | tf_op jit(solution)/shard_map/slice | solution.py:81
  411.4 4.6 %fusion = f32[1,3,8192]{1,2,0:T(8,128)} fusion(f32[4,8192]{0,1:T(8,128)S(1)} %copy-done.1, f32[8192]{0:T(1024)S(1)} %slice_reduce_fusion), kind=kLoop, calls=%fused_computation.15 | loop fusion | flops 24576 | bytes 229376 | tf_op jit(solution)/shard_map/broadcast_in_dim | solution.py:81
  415.9 3.5 copy.104
  (66 shorter events, 3.8 us)
Async XLA Ops:
  6.5 121.1 %copy-start = (bf16[1,8,128,128]{3,2,1,0:T(8,128)(2,1)S(1)}, bf16[1,8,128,128]{3,2,1,0:T(8,128)(2,1)}, u32[]{:S(2)}) copy-start(bf16[1,8,128,128]{3,2,1,0:T(8,128)(2,1)} %param.27) | copy-start | bytes 786436
  6.5 5.2 %copy-start.6 = (f32[1,3,8192]{2,0,1:T(1,128)S(1)}, f32[1,3,8192]{2,0,1:T(1,128)}, u32[]{:S(2)}) copy-start(f32[1,3,8192]{2,0,1:T(1,128)} %param.15) | copy-start | bytes 294916
  18.2 61.4 %copy-start.12 = (s32[1,128]{1,0:T(1,128)S(1)}, s32[1,128]{1,0:T(1,128)}, u32[]{:S(2)}) copy-start(s32[1,128]{1,0:T(1,128)} %param.22) | copy-start | bytes 1540
  18.2 74.1 %copy-start.13 = (s32[1,8]{1,0:T(1,128)S(1)}, s32[1,8]{1,0:T(1,128)}, u32[]{:S(2)}) copy-start(s32[1,8]{1,0:T(1,128)} %param.26) | copy-start | bytes 100
  18.2 74.1 %copy-start.3 = (s32[1,8,1024]{2,1,0:T(8,128)S(1)}, s32[1,8,1024]{2,1,0:T(8,128)}, u32[]{:S(2)}) copy-start(s32[1,8,1024]{2,1,0:T(8,128)} %param.19) | copy-start | bytes 98308
  18.3 74.2 %copy-start.2 = (s32[1,128,128]{2,1,0:T(8,128)S(1)}, s32[1,128,128]{2,1,0:T(8,128)}, u32[]{:S(2)}) copy-start(s32[1,128,128]{2,1,0:T(8,128)} %param.21) | copy-start | bytes 196612
  18.3 74.3 %copy-start.4 = (f32[1,64,3,128]{3,1,2,0:T(8,128)S(1)}, f32[1,64,3,128]{3,1,2,0:T(8,128)}, u32[]{:S(2)}) copy-start(f32[1,64,3,128]{3,1,2,0:T(8,128)} %param.24) | copy-start | bytes 294916
  18.3 74.4 %copy-start.5 = (f32[1,64,3,128]{3,1,2,0:T(8,128)S(1)}, f32[1,64,3,128]{3,1,2,0:T(8,128)}, u32[]{:S(2)}) copy-start(f32[1,64,3,128]{3,1,2,0:T(8,128)} %param.23) | copy-start | bytes 294916
  79.6 47.1 %copy-start.14 = (s32[1,8]{1,0:T(1,128)S(1)}, s32[1,8]{1,0:T(1,128)}, u32[]{:S(2)}) copy-start(s32[1,8]{1,0:T(1,128)} %param.25) | copy-start | bytes 100
  85.1 41.7 %all-to-all-start = ((bf16[8,32,3,128]{3,1,2,0:T(8,128)(2,1)}), bf16[8,32,3,128]{3,1,2,0:T(8,128)(2,1)S(1)}, u32[]{:S(2)}, u32[]{:S(2)}) async-start(bf16[8,32,3,128]{3,1,2,0:T(8,128)(2,1)} %copy.94), calls=%async_computation | async-start | bytes 393216 | tf_op jit(solution)/shard_map/all_to_all | solution.py:47
  123.8 11.9 %copy-start.8 = (f32[24,24]{1,0:T(8,128)S(1)}, f32[24,24]{1,0:T(8,128)}, u32[]{:S(2)}) copy-start(f32[24,24]{1,0:T(8,128)} %param.18) | copy-start | bytes 6916
  123.8 11.9 %copy-start.9 = (f32[1,1024]{1,0:T(1,128)S(1)}, f32[1,1024]{1,0:T(1,128)}, u32[]{:S(2)}) copy-start(f32[1,1024]{1,0:T(1,128)} %param.20) | copy-start | bytes 12292
  123.8 12.2 %copy-start.10 = (s32[1,512]{1,0:T(1,128)S(1)}, s32[1,512]{1,0:T(1,128)}, u32[]{:S(2)}) copy-start(s32[1,512]{1,0:T(1,128)} %param.28) | copy-start | bytes 6148
  123.8 12.3 %copy-start.11 = (s32[1,512]{1,0:T(1,128)S(1)}, s32[1,512]{1,0:T(1,128)}, u32[]{:S(2)}) copy-start(s32[1,512]{1,0:T(1,128)} %param.29) | copy-start | bytes 6148
  129.7 17.1 %all-to-all-start.1 = ((f32[8,32,3,128]{3,1,2,0:T(8,128)}), f32[8,32,3,128]{3,1,2,0:T(8,128)S(1)}, u32[]{:S(2)}, u32[]{:S(2)}) async-start(f32[8,32,3,128]{3,1,2,0:T(8,128)} %copy.99), calls=%async_computation.1 | async-start | bytes 786432 | tf_op jit(solution)/shard_map/all_to_all | solution.py:67
  135.7 237.1 %all-reduce.2.cloned.1.call-start = ((), (), s32[]{:S(2)}) async-start(), calls=%async_computation.2 | async-start | bytes 8388608 | tf_op jit(solution)/shard_map/psum | solution.py:74
  154.9 133.1 %copy-start.7 = (f32[1,8192]{1,0:T(1,128)S(1)}, f32[1,8192]{1,0:T(1,128)}, u32[]{:S(2)}) copy-start(f32[1,8192]{1,0:T(1,128)} %param.17) | copy-start | bytes 98308
  382.6 9.8 %collective-permute-start = (f32[4,512]{0,1:T(8,128)S(1)}, f32[4,512]{0,1:T(8,128)S(1)}, u32[]{:S(2)}, u32[]{:S(2)}) collective-permute-start(f32[4,512]{0,1:T(8,128)S(1)} %bitcast.113), channel_id=1, source_target_pairs={{4,0},{8,4},{12,8},{16,12},{20,16},{24,20},{28,24},{5,1},{9,5},{13... | collective-permute-start | bytes 24584 | tf_op jit(solution)/shard_map/ppermute | solution.py:12
  387.1 12.4 %collective-permute-start.1 = (f32[4,512]{0,1:T(8,128)S(1)}, f32[4,512]{0,1:T(8,128)S(1)}, u32[]{:S(2)}, u32[]{:S(2)}) collective-permute-start(f32[4,512]{0,1:T(8,128)S(1)} %bitcast.112), channel_id=1, source_target_pairs={{0,4},{4,8},{8,12},{12,16},{16,20},{20,24},{24,28},{1,5},{5,9},{9,... | collective-permute-start | bytes 24584 | tf_op jit(solution)/shard_map/ppermute | solution.py:12
  406.7 4.6 %copy-start.1 = (f32[4,8192]{0,1:T(8,128)S(1)}, f32[4,8192]{0,1:T(8,128)}, u32[]{:S(2)}) copy-start(f32[4,8192]{0,1:T(8,128)} %scatter_custom_fusion.4) | copy-start | bytes 393220
Sparse Core Ops, SparseCore 0:
  288.2 84.5 all-reduce.1
where the time goes:
time: 427 us; the launch traced here: 426 us
  other arithmetic  166 us (39%)
  local copies, waits for them, and re-layouts  134 us (31%)
  waiting for transfers between devices  93.3 us (22%)
  starting transfers between devices  19.3 us (5%)
  between operations  13.9 us (3%)
    scatter-add x1, other arithmetic, on_device(): jnp.zeros((3, nodes_all), jnp.float32).at[:, node_index].add(node_terms)  133 us
    psum x1, waiting for transfers between devices, on_device(): own = lax.psum(local_sum, 'rep')  82.1 us
    gather x2, local copies, waits for them, and re-layouts, on_device(): jnp.take(positions, surf, axis=1)  61.3 us
    gather x2, local copies, waits for them, and re-layouts, on_device(): local = moved[:, corner_points].reshape(24, -1)  32.8 us
    scatter-add x2, other arithmetic, on_device(): full.at[:, upper_nodes].add(from_upper).at[:, lower_nodes].add(from_lower)  14.3 us
    all_to_all x1, waiting for transfers between devices, on_device(): lax.all_to_all(partial_force, 'dom', split_axis=0, concat_axis=0, tiled=T...  10.7 us
    unnamed x36, local copies, waits for them, and re-layouts  8.94 us
  transfers between devices with their start and end apart: 5, of which 3 were waited for; matrix products, arithmetic and copies ran while one was open for 11% of the time, Pallas kernels for 0%

commit v1 on v0

v1 whole, which is shorter than its diff:
```python
import functools

import jax
import jax.numpy as jnp
from jax import lax
from jax.experimental import pallas as pl
from jax.experimental.pallas import tpu as pltpu
from jax.sharding import PartitionSpec as P

penalty = 4.0
lanes = 128
wide = 256
rowwise = lax.GatherDimensionNumbers(
    offset_dims=(),
    collapsed_slice_dims=(1,),
    start_index_map=(1,),
    operand_batching_dims=(0,),
    start_indices_batching_dims=(0,),
)
vmem = pl.BlockSpec(memory_space=pltpu.VMEM)
smem = pl.BlockSpec(memory_space=pltpu.SMEM)


def call(body, out_shape, in_specs, out_specs, scratch, flops):
    return pl.pallas_call(
        body,
        out_shape=out_shape,
        in_specs=in_specs,
        out_specs=out_specs,
        scratch_shapes=scratch,
        compiler_params=pltpu.CompilerParams(vmem_limit_bytes=32 * 1024 * 1024),
        cost_estimate=pl.CostEstimate(flops=flops, bytes_accessed=1 << 20, transcendentals=0),
    )


def lookup(rows_of, table_rows, wanted, comps, unroll=8):
    low = [(nodes & (lanes - 1))[..., None] for nodes in wanted]
    high = [nodes >> 7 for nodes in wanted]

    def step(r, held):
        rows = [jnp.broadcast_to(row, wanted[0].shape) for row in rows_of(r)]
        new = []
        for v in range(len(wanted)):
            here = high[v] == r
            for c in range(comps):
                found = lax.gather(
                    rows[c], low[v], rowwise, (1, 1), mode=lax.GatherScatterMode.PROMISE_IN_BOUNDS
                )
                new.append(jnp.where(here, found, held[v * comps + c]))
        return tuple(new)

    start = tuple(jnp.zeros(wanted[0].shape, jnp.float32) for _ in range(len(wanted) * comps))
    flat = lax.fori_loop(0, table_rows, step, start, unroll=unroll)
    return [flat[v * comps : (v + 1) * comps] for v in range(len(wanted))]


def add_at_nodes(total_ref, nodes, values, tops):
    count = nodes.shape[0]
    comps = len(values)
    top_row = lax.broadcasted_iota(jnp.int32, (tops, lanes), 0)
    low_row = lax.broadcasted_iota(jnp.int32, (wide, lanes), 0)
    top = nodes >> 8
    low = nodes & (wide - 1)
    coarse = [v.astype(jnp.bfloat16).astype(jnp.float32) for v in values]
    fine = [v - w for v, w in zip(values, coarse)]
    left, right = [], []
    for i in range(count):
        match = top_row == top[i : i + 1]
        pieces = [
            jnp.where(match, v[i : i + 1], 0.0).astype(jnp.bfloat16) for v in coarse + fine
        ]
        left.append(jnp.concatenate(pieces, axis=0))
        right.append(jnp.where(low_row == low[i : i + 1], 1.0, 0.0).astype(jnp.bfloat16))
    both = lax.dot_general(
        jnp.concatenate(left, axis=1),
        jnp.concatenate(right, axis=1),
        (((1,), (1,)), ((), ())),
        preferred_element_type=jnp.float32,
    )
    summed = both[: comps * tops] + both[comps * tops :]
    for c in range(comps):
        for half in range(2):
            at = (c * 2 + half) * tops
            total_ref[at : at + tops] += summed[
                c * tops : (c + 1) * tops, half * lanes : (half + 1) * lanes
            ]


def pack_kernel(cap, region_ref, slot_ref, coords_ref, disp_ref, surf_ref, out_ref, stage):
    parts, rows, _ = out_ref.shape
    nblk = surf_ref.shape[1]
    tiles = slot_ref.shape[1]
    table_rows = coords_ref.shape[2] // lanes

    def rows_of(r):
        at = pl.ds(pl.multiple_of(r * lanes, lanes), lanes)
        here = coords_ref[0, :, at] + disp_ref[0, :, at]
        return [here[c : c + 1] for c in range(3)]

    lane = lax.broadcasted_iota(jnp.int32, (rows - 3 * cap, lanes), 1)
    line = lax.broadcasted_iota(jnp.int32, (rows - 3 * cap, lanes), 0)
    tail = jnp.zeros((rows - 3 * cap, lanes), jnp.float32)
    for t in range(tiles):
        tail = jnp.where((lane == t) & (line == 0), slot_ref[0, t].astype(jnp.float32), tail)
    for q in range(nblk // cap):
        stage[q, 3 * cap :] = tail
    empty = jnp.concatenate([jnp.zeros((3 * cap, lanes), jnp.float32), tail], axis=0)
    for j in range(parts):
        out_ref[j] = empty.astype(jnp.bfloat16)
    group = 4
    for g in range(nblk // (8 * group)):
        first = g * group * 8
        wanted = [surf_ref[0, first + 8 * v : first + 8 * v + 8] for v in range(group)]
        found = lookup(rows_of, table_rows, wanted, 3)
        for v in range(group):
            for part in range(0, 8, min(cap, 8)):
                b = first + 8 * v + part
                size = min(cap, 8)
                for c in range(3):
                    at = c * cap + b % cap
                    stage[b // cap, at : at + size] = found[v][c][part : part + size]
    for q in range(nblk // cap):
        out_ref[region_ref[0, q * cap]] = stage[q].astype(jnp.bfloat16)


def element_kernel(disp_ref, stiff_ref, modulus_ref, nodes_ref, out_ref, local):
    corners, count = nodes_ref.shape[1:]
    nodes_all = disp_ref.shape[2]

    def rows_of(r):
        here = disp_ref[0, :, pl.ds(pl.multiple_of(r * lanes, lanes), lanes)]
        return [here[c : c + 1] for c in range(3)]

    group = 4
    for g in range(count // (lanes * group)):
        cuts = [slice((g * group + v) * lanes, (g * group + v + 1) * lanes) for v in range(group)]
        found = lookup(rows_of, nodes_all // lanes, [nodes_ref[0, :, cut] for cut in cuts], 3)
        for v, cut in enumerate(cuts):
            for c in range(3):
                local[c * corners : (c + 1) * corners, cut] = found[v][c]
    force = jnp.dot(
        stiff_ref[...],
        local[...],
        precision=lax.Precision.HIGHEST,
        preferred_element_type=jnp.float32,
    )
    local[...] = -(force * modulus_ref[...])
    out_ref[...] = jnp.zeros_like(out_ref)

    def spread(g, _):
        cut = pl.ds(pl.multiple_of(g * lanes, lanes), lanes)
        values = [local[c * corners : (c + 1) * corners, cut] for c in range(3)]
        add_at_nodes(out_ref, nodes_ref[0, :, cut], values, nodes_all // wide)
        return 0

    lax.fori_loop(0, count // lanes, spread, 0)


def tile_kernel(cap, slot_ref, face_ref, got_ref, pos_ref, normal_ref, weight_ref, out_ref, slots_ref, flat):
    parts, rows, _ = got_ref.shape
    tiles = slot_ref.shape[1]
    for j in range(parts):
        flat[j * rows : (j + 1) * rows] = got_ref[j].astype(jnp.float32)
    slots_ref[...] = jnp.concatenate(
        [flat[j * rows + 3 * cap : j * rows + 3 * cap + 1] for j in range(parts)], axis=0
    ).astype(jnp.int32)
    forces = []
    for t in range(tiles):
        slot = slot_ref[0, t]
        at = (slot // cap) * rows + slot % cap
        x = jnp.concatenate([flat[pl.ds(at + c * cap, 1)] for c in range(3)], axis=0)
        weight = weight_ref[0, t]
        normal = normal_ref[0, face_ref[0, t]]
        interp = lax.dot_general(
            x.astype(jnp.bfloat16),
            weight,
            (((1,), (1,)), ((), ())),
            preferred_element_type=jnp.float32,
        )
        gap = jnp.sum(normal * (interp - pos_ref[0, face_ref[0, t]]), axis=0, keepdims=True)
        push = (penalty * jnp.maximum(-gap, 0.0) * normal).astype(jnp.bfloat16)
        forces.append(jnp.dot(push, weight, preferred_element_type=jnp.float32))
    all_forces = jnp.concatenate(forces, axis=0)
    for j in range(parts):
        out_ref[j] = all_forces


def contact_kernel(
    cap, tiles, slots_ref, region_ref, back_ref, surf_ref, part_ref, mass_ref, lo_ref, hi_ref,
    out_ref, share_lo_ref, share_hi_ref, run_of, node_rows, force_rows,
):
    parts = back_ref.shape[0]
    nblk = surf_ref.shape[1]
    nodes_all = mass_ref.shape[1]
    tops = nodes_all // wide
    me = lax.axis_index("dom")
    out_ref[...] = part_ref[...]
    node_rows[...] = jnp.full_like(node_rows, -1)

    def clear(j, _):
        run_of[j] = 0
        return 0

    lax.fori_loop(0, parts, clear, 0)
    for q in range(nblk // cap):
        run_of[region_ref[0, q * cap]] = q * cap

    def pick(j, filled):
        for t in range(tiles):
            slot = slots_ref[j, t]
            block = run_of[j] + slot % cap
            node_rows[pl.ds(filled, 1)] = surf_ref[0, pl.ds(block, 1)]
            for c in range(3):
                force_rows[c, pl.ds(filled, 1)] = back_ref[j, t * 3 + c : t * 3 + c + 1]
            filled = filled + jnp.where(slot // cap == me, 1, 0)
        return filled

    filled = lax.fori_loop(0, parts, pick, 0)
    node_rows[pl.ds(filled, 1)] = jnp.full((1, lanes), -1, jnp.int32)

    def spread(g, _):
        at = pl.ds(pl.multiple_of(g * 8, 8), 8)
        add_at_nodes(out_ref, node_rows[at], [force_rows[c, at] for c in range(3)], tops)
        return 0

    lax.fori_loop(0, (filled + 7) // 8, spread, 0)

    def rows_of(r):
        base = (r & 1) * tops + (r >> 1)
        rows = [out_ref[pl.ds(c * 2 * tops + base, 1)] for c in range(3)]
        return rows + [mass_ref[:, pl.ds(pl.multiple_of(r * lanes, lanes), lanes)]]

    shared = lo_ref.shape[1] // lanes
    wanted = jnp.concatenate(
        [ref[:, k * lanes : (k + 1) * lanes] for ref in (lo_ref, hi_ref) for k in range(shared)],
        axis=0,
    )
    found = lookup(rows_of, nodes_all // lanes, [wanted], 4)[0]
    for c in range(4):
        share_lo_ref[c * shared : (c + 1) * shared] = found[c][:shared]
        share_hi_ref[c * shared : (c + 1) * shared] = found[c][shared:]


def share_kernel(part_ref, mass_ref, up_ref, down_ref, lo_ref, hi_ref, out_ref, out_mass_ref, total):
    nodes_all = mass_ref.shape[1]
    tops = nodes_all // wide
    size = 3 * 2 * tops
    total[:size] = part_ref[...]
    for r in range(nodes_all // lanes):
        at = size + (r & 1) * tops + (r >> 1)
        total[at : at + 1] = mass_ref[:, r * lanes : (r + 1) * lanes]
    shared = lo_ref.shape[1] // lanes
    wanted = jnp.concatenate(
        [ref[:, k * lanes : (k + 1) * lanes] for ref in (hi_ref, lo_ref) for k in range(shared)],
        axis=0,
    )
    values = [
        jnp.concatenate(
            [ref[c * shared : (c + 1) * shared] for ref in (up_ref, down_ref)], axis=0
        )
        for c in range(4)
    ]
    add_at_nodes(total, wanted, values, tops)
    out_ref[...] = total[:size]
    out_mass_ref[...] = total[size:]


def accel_kernel(*refs):
    mass_ref, sums, out_ref, quotient = refs[0], refs[1:-2], refs[-2], refs[-1]
    nodes_all = out_ref.shape[2]
    tops = nodes_all // wide
    terms = [ref[...] for ref in sums]
    while len(terms) > 1:
        terms = [a + b for a, b in zip(terms[::2], terms[1::2])]
    mass = mass_ref[...]
    for c in range(3):
        at = slice(c * 2 * tops, (c + 1) * 2 * tops)
        quotient[at] = terms[0][at] / mass
    for r in range(nodes_all // lanes):
        at = (r & 1) * tops + (r >> 1)
        for c in range(3):
            row = c * 2 * tops + at
            out_ref[0, c : c + 1, r * lanes : (r + 1) * lanes] = quotient[row : row + 1]


def shifted(block, axis, distance):
    devices = range(lax.axis_size(axis))
    route = [(i - distance, i) for i in devices if i - distance in devices]
    return lax.ppermute(block, axis, route)


def on_device(
    coords,
    disp,
    mass,
    stiffness,
    elem_nodes,
    modulus,
    surf_nodes,
    block_region,
    face_pos,
    face_normal,
    tile_slot,
    tile_face,
    tile_weight,
    shared_lo,
    shared_hi,
):
    parts = lax.axis_size("dom")
    mates = lax.axis_size("rep")
    nodes_all = disp.shape[2]
    nblk = surf_nodes.shape[1]
    tiles = tile_slot.shape[1]
    cap = max(2, 2 * nblk // parts)
    rows = (3 * cap + 1 + 15) // 16 * 16
    tops = nodes_all // wide
    size = 3 * 2 * tops
    shared = shared_lo.shape[1] // lanes
    f32 = jnp.float32

    outgoing = call(
        functools.partial(pack_kernel, cap),
        jax.ShapeDtypeStruct((parts, rows, lanes), jnp.bfloat16),
        [smem, smem, vmem, vmem, vmem],
        vmem,
        [pltpu.VMEM((nblk // cap, rows, lanes), f32)],
        1 << 30,
    )(block_region, tile_slot, coords, disp, surf_nodes)
    arrived = lax.all_to_all(outgoing, "dom", split_axis=0, concat_axis=0, tiled=True)

    part = call(
        element_kernel,
        jax.ShapeDtypeStruct((size, lanes), f32),
        [vmem] * 4,
        vmem,
        [pltpu.VMEM((24, modulus.shape[1]), f32)],
        1 << 32,
    )(disp, stiffness, modulus, elem_nodes)

    forces, slots = call(
        functools.partial(tile_kernel, cap),
        (
            jax.ShapeDtypeStruct((parts, tiles * 3, lanes), f32),
            jax.ShapeDtypeStruct((parts, lanes), jnp.int32),
        ),
        [smem, smem, vmem, vmem, vmem, vmem],
        (vmem, vmem),
        [pltpu.VMEM((parts * rows, lanes), f32)],
        1 << 28,
    )(tile_slot, tile_face, arrived, face_pos, face_normal, tile_weight)
    back = lax.all_to_all(forces, "dom", split_axis=0, concat_axis=0, tiled=True)

    picked = (parts * tiles + 1 + 7) // 8 * 8
    share = jax.ShapeDtypeStruct((4 * shared, lanes), f32)
    part, share_lo, share_hi = call(
        functools.partial(contact_kernel, cap, tiles),
        (jax.ShapeDtypeStruct((size, lanes), f32), share, share),
        [smem, smem] + [vmem] * 6,
        (vmem, vmem, vmem),
        [
            pltpu.SMEM((parts,), jnp.int32),
            pltpu.VMEM((picked, lanes), jnp.int32),
            pltpu.VMEM((3, picked, lanes), f32),
        ],
        1 << 28,
    )(slots, block_region, back, surf_nodes, part, mass, shared_lo, shared_hi)
    from_upper = shifted(share_lo, "dom", -1)
    from_lower = shifted(share_hi, "dom", 1)

    own, own_mass = call(
        share_kernel,
        (jax.ShapeDtypeStruct((size, lanes), f32), jax.ShapeDtypeStruct((2 * tops, lanes), f32)),
        [vmem] * 6,
        (vmem, vmem),
        [pltpu.VMEM((4 * 2 * tops, lanes), f32)],
        1 << 28,
    )(part, mass, from_upper, from_lower, shared_lo, shared_hi)
    others = [
        lax.ppermute(own, "rep", [(i, i ^ k) for i in range(mates)]) for k in range(1, mates)
    ]
    return call(
        accel_kernel,
        jax.ShapeDtypeStruct((1, 3, nodes_all), f32),
        [vmem] * (2 + len(others)),
        vmem,
        [pltpu.VMEM((size, lanes), f32)],
        1 << 24,
    )(own_mass, own, *others)


def solution(mesh):
    in_specs = (
        P("dom", None, None),
        P("dom", None, None),
        P("dom", None),
        P(),
        P("dom", None, "rep"),
        P("dom", "rep"),
        P("dom", None, None),
        P("dom", None),
        P("dom", None, None, None),
        P("dom", None, None, None),
        P("dom", "rep"),
        P("dom", "rep"),
        P("dom", "rep", None, None),
        P("dom", None),
        P("dom", None),
    )
    out_specs = P("dom", None, None)
    return jax.shard_map(
        on_device, mesh=mesh, in_specs=in_specs, out_specs=out_specs, check_vma=False
    )
```

time: 427 us -> 61.8 us (0.14)
  the two profiles are of different devices: /device:TPU:0 before, /device:TPU:9 now
where the time goes in v1:
time: 61.8 us; the launch traced here: 61.5 us
  Pallas kernels  23.1 us (37%)
  starting transfers between devices  22 us (36%)
  waiting for transfers between devices  13.5 us (22%)
  local copies, waits for them, and re-layouts  2.75 us (4%)
    pallas_call x1, Pallas kernels, on_device(): call(functools.partial(pack_kernel, cap), jax.ShapeDtypeStruct((parts, ro...  9.84 us
    pallas_call x1, Pallas kernels, on_device(): call(element_kernel, jax.ShapeDtypeStruct((size, lanes), f32), [vmem] * 4...  7.42 us
    all_to_all x1, starting transfers between devices, on_device(): lax.all_to_all(forces, 'dom', split_axis=0, concat_axis=0, tiled=True)  5.88 us
    all_to_all x1, starting transfers between devices, on_device(): lax.all_to_all(outgoing, 'dom', split_axis=0, concat_axis=0, tiled=True)  5.85 us
    all_to_all x1, waiting for transfers between devices, on_device(): lax.all_to_all(outgoing, 'dom', split_axis=0, concat_axis=0, tiled=True)  5.57 us
    ppermute x2, starting transfers between devices, shifted(): return lax.ppermute(block, axis, route)  5.28 us
    ppermute x3, waiting for transfers between devices, on_device(): lax.ppermute(own, 'rep', [(i, i ^ k) for i in range(mates)])  5.19 us
    ppermute x3, starting transfers between devices, on_device(): lax.ppermute(own, 'rep', [(i, i ^ k) for i in range(mates)])  4.97 us
  transfers between devices with their start and end apart: 7, of which 4 were waited for; matrix products, arithmetic and copies ran while one was open for 0% of the time, Pallas kernels for 12%

profile of v1, /device:TPU:9, one launch (start us, length us, event | category | flops | bytes accessed | tf_op | source)
XLA Modules:
  0.0 61.5 jit_solution(14025068741638561057)
XLA Ops:
  0.0 1.0 %copy.17.disp_ref = f32[1,3,8192]{2,1,0:T(4,128)S(1)} copy(f32[1,3,8192]{2,0,1:T(1,128)} %param.16) | data formatting | bytes 196608 | tf_op args[1]
  1.0 0.0 copy-start.1
  1.0 0.0 copy-start.8
  1.0 0.0 copy-start.10
  1.0 0.1 copy.16.coords_ref
  1.1 0.7 %copy-done.1 = s32[1,128,128]{2,1,0:T(8,128)S(1)} copy-done((s32[1,128,128]{2,1,0:T(8,128)S(1)}, s32[1,128,128]{2,1,0:T(8,128)}, u32[]{:S(2)}) %copy-start.1) | copy-done | bytes 65560
  1.9 9.8 %shard_map.145 = bf16[8,112,128]{2,1,0:T(8,128)(2,1)} custom-call(s32[1,128]{1,0:T(1,128)S(1)} %copy-done.10, s32[1,8]{1,0:T(1,128)S(1)} %copy-done.8, f32[1,3,8192]{2,1,0:T(4,128)S(1)} %copy.16.coords_ref, f32[1,3,8192]{2,1,0:T(4,128)S(1)} %copy.17.disp_ref, s32[1,128,128]{2,1,0:T(8,128)S(1)} %copy-done.1), custom_call_target="tpu_custom_call" | custom-call | flops 1073741824 | bytes 1048576 | tf_op jit(solution)/shard_map/pallas_call | solution.py:321
  11.7 5.9 %all-to-all-start = ((bf16[8,112,128]{2,1,0:T(8,128)(2,1)}), bf16[8,112,128]{2,1,0:T(8,128)(2,1)S(1)}, u32[]{:S(2)}, u32[]{:S(2)}) async-start(bf16[8,112,128]{2,1,0:T(8,128)(2,1)} %shard_map.145), calls=%async_computation | async-start | bytes 458752 | tf_op jit(solution)/shard_map/all_to_all | solution.py:329
  17.6 0.1 copy.18.pos_ref
  17.6 0.0 copy-start.9
  17.7 0.1 copy.19.normal_ref
  17.7 5.6 %all-to-all-done.got_ref = bf16[8,112,128]{2,1,0:T(8,128)(2,1)S(1)} async-done(((bf16[8,112,128]{2,1,0:T(8,128)(2,1)}), bf16[8,112,128]{2,1,0:T(8,128)(2,1)S(1)}, u32[]{:S(2)}, u32[]{:S(2)}) %all-to-all-start) | async-done | bytes 229408 | tf_op jit(solution)/shard_map/all_to_all | solution.py:329
  23.3 2.6 %shard_map.146 = (f32[8,24,128]{2,1,0:T(8,128)}, s32[8,128]{1,0:T(8,128)S(1)}) custom-call(s32[1,8]{1,0:T(1,128)S(1)} %copy-done.8, s32[1,8]{1,0:T(1,128)S(1)} %copy-done.9, bf16[8,112,128]{2,1,0:T(8,128)(2,1)S(1)} %all-to-all-done.got_ref, f32[1,64,3,128]{3,2,1,0:T(4,128)S(1)} %copy.18.pos_ref, f32[1,64,3,128]{3,2,1,0:T(4,128)S(1)} %copy.19.normal_ref, ...), custom_call_target="tpu_custom_call" | custom-call | flops 268435456 | bytes 1048576 | tf_op jit(solution)/shard_map/pallas_call | solution.py:340
  25.9 5.9 %all-to-all-start.1 = ((f32[8,24,128]{2,1,0:T(8,128)}), f32[8,24,128]{2,1,0:T(8,128)S(1)}, u32[]{:S(2)}, u32[]{:S(2)}) async-start(f32[8,24,128]{2,1,0:T(8,128)} %get-tuple-element.13), calls=%async_computation.1 | async-start | bytes 196608 | tf_op jit(solution)/shard_map/all_to_all | solution.py:351
  31.8 0.0 copy-start.3
  31.8 0.0 copy-start.6
  31.8 0.0 copy-start.7
  31.8 7.4 %shard_map.147.part_ref = f32[192,128]{1,0:T(8,128)S(1)} custom-call(f32[1,3,8192]{2,1,0:T(4,128)S(1)} %copy.17.disp_ref, f32[24,24]{1,0:T(8,128)S(1)} %copy-done.4, f32[1,1024]{1,0:T(1,128)S(1)} %copy-done.5, s32[1,8,1024]{2,1,0:T(8,128)S(1)} %copy-done.2), custom_call_target="tpu_custom_call" | custom-call | flops 4294967296 | bytes 1048576 | tf_op jit(solution)/shard_map/pallas_call | solution.py:331
  39.3 0.0 all-to-all-done.1.back_ref
  39.3 2.8 %shard_map.148 = (f32[192,128]{1,0:T(8,128)S(1)}, f32[16,128]{1,0:T(8,128)S(1)}, f32[16,128]{1,0:T(8,128)S(1)}) custom-call(s32[8,128]{1,0:T(8,128)S(1)} %get-tuple-element.12.slots_ref, s32[1,128]{1,0:T(1,128)S(1)} %copy-done.10, f32[8,24,128]{2,1,0:T(8,128)S(1)} %all-to-all-done.1.back_ref, s32[1,128,128]{2,1,0:T(8,128)S(1)} %copy-done.1, ...), custom_call_target="tpu_custom_call" | custom-call | flops 268435456 | bytes 1048576 | tf_op jit(solution)/shard_map/pallas_call | solution.py:355
  42.1 2.7 %collective-permute-start = (f32[16,128]{1,0:T(8,128)S(1)}, f32[16,128]{1,0:T(8,128)S(1)}, u32[]{:S(2)}, u32[]{:S(2)}) collective-permute-start(f32[16,128]{1,0:T(8,128)S(1)} %get-tuple-element.15), channel_id=1, source_target_pairs={{4,0},{8,4},{12,8},{16,12},{20,16},{24,20},{28,24},{5,1},{9,5},{13... | collective-permute-start | bytes 24584 | tf_op jit(solution)/shard_map/ppermute | solution.py:289
  44.8 2.6 %collective-permute-start.1 = (f32[16,128]{1,0:T(8,128)S(1)}, f32[16,128]{1,0:T(8,128)S(1)}, u32[]{:S(2)}, u32[]{:S(2)}) collective-permute-start(f32[16,128]{1,0:T(8,128)S(1)} %get-tuple-element.16), channel_id=1, source_target_pairs={{0,4},{4,8},{8,12},{12,16},{16,20},{20,24},{24,28},{1,5},{5,9},{9,... | collective-permute-start | bytes 24584 | tf_op jit(solution)/shard_map/ppermute | solution.py:289
  47.4 2.7 %collective-permute-done.1.down_ref = f32[16,128]{1,0:T(8,128)S(1)} collective-permute-done((f32[16,128]{1,0:T(8,128)S(1)}, f32[16,128]{1,0:T(8,128)S(1)}, u32[]{:S(2)}, u32[]{:S(2)}) %collective-permute-start.1) | collective-permute-done | bytes 8224 | tf_op jit(solution)/shard_map/ppermute | solution.py:289
  50.1 0.4 shard_map.149
  50.5 4.5 %collective-permute-start.4 = (f32[192,128]{1,0:T(8,128)S(1)}, f32[192,128]{1,0:T(8,128)S(1)}, u32[]{:S(2)}, u32[]{:S(2)}) collective-permute-start(f32[192,128]{1,0:T(8,128)S(1)} %get-tuple-element.18.refs_1_), channel_id=1, source_target_pairs={{0,3},{1,2},{2,1},{3,0},{4,7},{5,6},{6,5},{7,4},{8,11},{9,10},{10,... | collective-permute-start | bytes 294920 | tf_op jit(solution)/shard_map/ppermute | solution.py:379
  55.0 0.3 collective-permute-start.3
  55.3 0.2 collective-permute-start.2
  55.5 3.1 %collective-permute-done.4.refs_4_ = f32[192,128]{1,0:T(8,128)S(1)} collective-permute-done((f32[192,128]{1,0:T(8,128)S(1)}, f32[192,128]{1,0:T(8,128)S(1)}, u32[]{:S(2)}, u32[]{:S(2)}) %collective-permute-start.4) | collective-permute-done | bytes 98336 | tf_op jit(solution)/shard_map/ppermute | solution.py:379
  58.6 2.1 %collective-permute-done.3.refs_3_ = f32[192,128]{1,0:T(8,128)S(1)} collective-permute-done((f32[192,128]{1,0:T(8,128)S(1)}, f32[192,128]{1,0:T(8,128)S(1)}, u32[]{:S(2)}, u32[]{:S(2)}) %collective-permute-start.3) | collective-permute-done | bytes 98336 | tf_op jit(solution)/shard_map/ppermute | solution.py:379
  60.7 0.0 collective-permute-done.2.refs_2_
  60.7 0.1 shard_map.150
  60.8 0.7 %copy.21 = f32[1,3,8192]{2,0,1:T(1,128)} copy(f32[1,3,8192]{2,1,0:T(4,128)S(1)} %shard_map.150) | data formatting | bytes 196608 | tf_op jit(solution)/shard_map/pallas_call | solution.py:381
  (21 shorter events, 0.0 us)
Async XLA Ops:
  0.0 1.0 %copy-start.11 = (f32[1,3,8192]{2,0,1:T(1,128)S(1)}, f32[1,3,8192]{2,0,1:T(1,128)}, u32[]{:S(2)}) copy-start(f32[1,3,8192]{2,0,1:T(1,128)} %param.15) | copy-start | bytes 294916
  1.0 0.8 %copy-start.1 = (s32[1,128,128]{2,1,0:T(8,128)S(1)}, s32[1,128,128]{2,1,0:T(8,128)}, u32[]{:S(2)}) copy-start(s32[1,128,128]{2,1,0:T(8,128)} %surf_ref.3) | copy-start | bytes 196612
  1.0 0.8 %copy-start.8 = (s32[1,8]{1,0:T(1,128)S(1)}, s32[1,8]{1,0:T(1,128)}, u32[]{:S(2)}) copy-start(s32[1,8]{1,0:T(1,128)} %slot_ref.3) | copy-start | bytes 100
  1.0 0.8 %copy-start.10 = (s32[1,128]{1,0:T(1,128)S(1)}, s32[1,128]{1,0:T(1,128)}, u32[]{:S(2)}) copy-start(s32[1,128]{1,0:T(1,128)} %region_ref.3) | copy-start | bytes 1540
  11.7 5.9 %copy-start.12 = (f32[1,64,3,128]{3,1,2,0:T(8,128)S(1)}, f32[1,64,3,128]{3,1,2,0:T(8,128)}, u32[]{:S(2)}) copy-start(f32[1,64,3,128]{3,1,2,0:T(8,128)} %param.23) | copy-start | bytes 294916
  11.7 5.9 %copy-start.13 = (f32[1,64,3,128]{3,1,2,0:T(8,128)S(1)}, f32[1,64,3,128]{3,1,2,0:T(8,128)}, u32[]{:S(2)}) copy-start(f32[1,64,3,128]{3,1,2,0:T(8,128)} %param.24) | copy-start | bytes 294916
  11.7 11.6 %all-to-all-start = ((bf16[8,112,128]{2,1,0:T(8,128)(2,1)}), bf16[8,112,128]{2,1,0:T(8,128)(2,1)S(1)}, u32[]{:S(2)}, u32[]{:S(2)}) async-start(bf16[8,112,128]{2,1,0:T(8,128)(2,1)} %shard_map.145), calls=%async_computation | async-start | bytes 458752 | tf_op jit(solution)/shard_map/all_to_all | solution.py:329
  17.6 5.8 %copy-start = (bf16[1,8,128,128]{3,2,1,0:T(8,128)(2,1)S(1)}, bf16[1,8,128,128]{3,2,1,0:T(8,128)(2,1)}, u32[]{:S(2)}) copy-start(bf16[1,8,128,128]{3,2,1,0:T(8,128)(2,1)} %weight_ref.1) | copy-start | bytes 786436
  17.6 5.7 %copy-start.9 = (s32[1,8]{1,0:T(1,128)S(1)}, s32[1,8]{1,0:T(1,128)}, u32[]{:S(2)}) copy-start(s32[1,8]{1,0:T(1,128)} %face_ref.1) | copy-start | bytes 100
  25.9 5.9 %copy-start.2 = (s32[1,8,1024]{2,1,0:T(8,128)S(1)}, s32[1,8,1024]{2,1,0:T(8,128)}, u32[]{:S(2)}) copy-start(s32[1,8,1024]{2,1,0:T(8,128)} %nodes_ref.1) | copy-start | bytes 98308
  25.9 5.9 %copy-start.4 = (f32[24,24]{1,0:T(8,128)S(1)}, f32[24,24]{1,0:T(8,128)}, u32[]{:S(2)}) copy-start(f32[24,24]{1,0:T(8,128)} %stiff_ref.1) | copy-start | bytes 6916
  25.9 5.9 %copy-start.5 = (f32[1,1024]{1,0:T(1,128)S(1)}, f32[1,1024]{1,0:T(1,128)}, u32[]{:S(2)}) copy-start(f32[1,1024]{1,0:T(1,128)} %modulus_ref.1) | copy-start | bytes 12292
  25.9 13.4 %all-to-all-start.1 = ((f32[8,24,128]{2,1,0:T(8,128)}), f32[8,24,128]{2,1,0:T(8,128)S(1)}, u32[]{:S(2)}, u32[]{:S(2)}) async-start(f32[8,24,128]{2,1,0:T(8,128)} %get-tuple-element.13), calls=%async_computation.1 | async-start | bytes 196608 | tf_op jit(solution)/shard_map/all_to_all | solution.py:351
  31.8 7.5 %copy-start.3 = (f32[1,8192]{1,0:T(1,128)S(1)}, f32[1,8192]{1,0:T(1,128)}, u32[]{:S(2)}) copy-start(f32[1,8192]{1,0:T(1,128)} %mass_ref.3) | copy-start | bytes 98308
  31.8 7.5 %copy-start.6 = (s32[1,512]{1,0:T(1,128)S(1)}, s32[1,512]{1,0:T(1,128)}, u32[]{:S(2)}) copy-start(s32[1,512]{1,0:T(1,128)} %lo_ref.3) | copy-start | bytes 6148
  31.8 7.5 %copy-start.7 = (s32[1,512]{1,0:T(1,128)S(1)}, s32[1,512]{1,0:T(1,128)}, u32[]{:S(2)}) copy-start(s32[1,512]{1,0:T(1,128)} %hi_ref.3) | copy-start | bytes 6148
  42.1 5.3 %collective-permute-start = (f32[16,128]{1,0:T(8,128)S(1)}, f32[16,128]{1,0:T(8,128)S(1)}, u32[]{:S(2)}, u32[]{:S(2)}) collective-permute-start(f32[16,128]{1,0:T(8,128)S(1)} %get-tuple-element.15), channel_id=1, source_target_pairs={{4,0},{8,4},{12,8},{16,12},{20,16},{24,20},{28,24},{5,1},{9,5},{13... | collective-permute-start | bytes 24584 | tf_op jit(solution)/shard_map/ppermute | solution.py:289
  44.8 5.3 %collective-permute-start.1 = (f32[16,128]{1,0:T(8,128)S(1)}, f32[16,128]{1,0:T(8,128)S(1)}, u32[]{:S(2)}, u32[]{:S(2)}) collective-permute-start(f32[16,128]{1,0:T(8,128)S(1)} %get-tuple-element.16), channel_id=1, source_target_pairs={{0,4},{4,8},{8,12},{12,16},{16,20},{20,24},{24,28},{1,5},{5,9},{9,... | collective-permute-start | bytes 24584 | tf_op jit(solution)/shard_map/ppermute | solution.py:289
  50.5 8.0 %collective-permute-start.4 = (f32[192,128]{1,0:T(8,128)S(1)}, f32[192,128]{1,0:T(8,128)S(1)}, u32[]{:S(2)}, u32[]{:S(2)}) collective-permute-start(f32[192,128]{1,0:T(8,128)S(1)} %get-tuple-element.18.refs_1_), channel_id=1, source_target_pairs={{0,3},{1,2},{2,1},{3,0},{4,7},{5,6},{6,5},{7,4},{8,11},{9,10},{10,... | collective-permute-start | bytes 294920 | tf_op jit(solution)/shard_map/ppermute | solution.py:379
  55.0 5.7 %collective-permute-start.3 = (f32[192,128]{1,0:T(8,128)S(1)}, f32[192,128]{1,0:T(8,128)S(1)}, u32[]{:S(2)}, u32[]{:S(2)}) collective-permute-start(f32[192,128]{1,0:T(8,128)S(1)} %get-tuple-element.18.refs_1_), channel_id=1, source_target_pairs={{0,2},{1,3},{2,0},{3,1},{4,6},{5,7},{6,4},{7,5},{8,10},{9,11},{10,... | collective-permute-start | bytes 294920 | tf_op jit(solution)/shard_map/ppermute | solution.py:379
  55.3 5.4 %collective-permute-start.2 = (f32[192,128]{1,0:T(8,128)S(1)}, f32[192,128]{1,0:T(8,128)S(1)}, u32[]{:S(2)}, u32[]{:S(2)}) collective-permute-start(f32[192,128]{1,0:T(8,128)S(1)} %get-tuple-element.18.refs_1_), channel_id=1, source_target_pairs={{0,1},{1,0},{2,3},{3,2},{4,5},{5,4},{6,7},{7,6},{8,9},{9,8},{10,11... | collective-permute-start | bytes 294920 | tf_op jit(solution)/shard_map/ppermute | solution.py:379
